TPU v7x, 32 devices: a whole 2x2x4 slice. The times are simulated.
32 devices in a mesh: seq: 4 (over y, x), head: 8 (over z, core).
Axes of the slice: x: 2, y: 2, z: 4, core: 2. Of those that a mesh axis runs over, the one named last changes fastest.
Arguments:
- query_rows: bfloat16 [4, 2048, 8192], P(None, 'seq', 'head'), may hold values from -6 to 6
- key_rows: bfloat16 [4, 2048, 8192], P(None, 'seq', 'head'), may hold values from -6 to 6
- value_rows: bfloat16 [4, 2048, 8192], P(None, 'seq', 'head'), may hold values from -6 to 6
- prior_state: float32 [4, 64, 128, 128], P(None, 'head'), may hold values from -256 to 256
- tree_query: bfloat16 [4, 256, 8192], P(None, 'seq', 'head'), may hold values from -6 to 6
- tree_key: bfloat16 [4, 256, 8192], P(None, 'seq', 'head'), may hold values from -6 to 6
- tree_value: bfloat16 [4, 256, 8192], P(None, 'seq', 'head'), may hold values from -12 to 12
- parents: int32 [4, 256], replicated, may hold values from 0 to 254, as said below
- out_weight: bfloat16 [8192, 8192], P('head', 'seq'), may hold values from -0.0625 to 0.0625
Outputs:
- prefill_out: bfloat16 [4, 2048, 8192], P(None, 'seq', 'head')
- verified: bfloat16 [1024, 8192], P('head', 'seq')
Inputs may be any that keep to these rules, and one draw needn't show every extreme that they name: parents[r, 0] is 0; for every node n >= 1, parents[r, n] lies between n - 4 and n - 1 and is at least 0.
All inputs are finite; a program needn't handle non-finite values.
Results may differ from a plain program's by a relative error of at most 0.023.
Values may be sent and summed in bfloat16 or wider, within the bound.
A program may use at most 128 MiB of HBM per device.

v0:
```python
import jax
import jax.numpy as jnp
from jax import lax
from jax.sharding import PartitionSpec as P

DH = 128
NODES = 256


epsilon = 1e-05


def head_norm(field):
    return field * lax.rsqrt(jnp.mean(field * field, axis=-1, keepdims=True) + epsilon)


def on_device(
    query_rows,
    key_rows,
    value_rows,
    prior_state,
    tree_query,
    tree_key,
    tree_value,
    parents,
    out_weight,
):
    requests, tokens, width = query_rows.shape
    heads_here = width // DH
    block = min(512, tokens)
    blocks = tokens // block
    seq_index = lax.axis_index("seq")
    seq_count = lax.axis_size("seq")
    pieces_dev = requests * heads_here // seq_count
    shape_five = (requests, blocks, block, heads_here, DH)
    q_blocks = query_rows.reshape(shape_five)
    k_blocks = key_rows.reshape(shape_five)
    v_blocks = value_rows.reshape(shape_five)
    block_states = jnp.einsum(
        "rnchd,rnche->rnhde", k_blocks, v_blocks, preferred_element_type=jnp.float32
    )
    span_state = jnp.sum(block_states, axis=1)
    leading = jnp.zeros_like(block_states)
    running = jnp.concatenate([leading, jnp.cumsum(block_states, axis=1)[:, :-1]], axis=1)
    scores = jnp.einsum(
        "rnbhd,rnchd->rnhbc", q_blocks, k_blocks, preferred_element_type=jnp.float32
    )
    causal = jnp.arange(block)[:, None] >= jnp.arange(block)[None, :]
    weights = jnp.where(causal, scores, 0.0).astype(jnp.bfloat16)
    inner = jnp.einsum("rnhbc,rnchd->rnbhd", weights, v_blocks, preferred_element_type=jnp.float32)
    empty_state = jnp.zeros_like(span_state)
    pieces_in = lax.all_gather(
        span_state[None].astype(jnp.bfloat16), "seq", axis=0, tiled=True
    ).astype(jnp.float32)
    earlier = empty_state
    whole = empty_state
    order = jnp.arange(pieces_in.shape[0])
    before = (order < seq_index)[:, None, None, None, None]
    earlier = earlier + jnp.sum(jnp.where(before, pieces_in, 0.0), axis=0)
    whole = whole + jnp.sum(pieces_in, axis=0)
    flat_total = whole.reshape(requests * heads_here, DH, DH)
    owned = lax.dynamic_slice_in_dim(flat_total, seq_index * pieces_dev, pieces_dev, 0)
    base_state = prior_state + earlier
    block_base = (base_state[:, None] + running).astype(jnp.bfloat16)
    context = jnp.einsum(
        "rnbhd,rnhde->rnbhe", q_blocks, block_base, preferred_element_type=jnp.float32
    )
    prefill_out = head_norm(context + inner).astype(jnp.bfloat16).reshape(requests, tokens, width)
    nodes_here = tree_query.shape[1]

    def to_owners(field):
        grouped = field.reshape(requests, nodes_here, heads_here, DH).transpose(0, 2, 1, 3)
        return grouped.reshape(seq_count, pieces_dev, nodes_here, DH)

    owner_query, owner_key, owner_value = (
        lax.all_to_all(to_owners(tree_query), "seq", split_axis=0, concat_axis=2, tiled=True),
        lax.all_to_all(to_owners(tree_key), "seq", split_axis=0, concat_axis=2, tiled=True),
        lax.all_to_all(to_owners(tree_value), "seq", split_axis=0, concat_axis=2, tiled=True),
    )
    owner_query = owner_query[0]
    owner_key = owner_key[0]
    owner_value = owner_value[0]
    flat_prior = prior_state.reshape(requests * heads_here, DH, DH)
    owned_prior = lax.dynamic_slice_in_dim(flat_prior, seq_index * pieces_dev, pieces_dev, 0)
    owned_total = (owned + owned_prior).astype(jnp.bfloat16)
    piece_ids = seq_index * pieces_dev + jnp.arange(pieces_dev)
    request_ids = piece_ids // heads_here
    own_parents = jnp.take(parents, request_ids, axis=0)
    node_ids = jnp.arange(NODES)
    links = (own_parents[:, :, None] == node_ids[None, None, :]) & (node_ids[None, :, None] >= 1)
    itself = (node_ids[:, None] == node_ids[None, :])[None]
    reach = (links | itself).astype(jnp.bfloat16)
    for level in range((NODES - 1).bit_length()):
        square = jnp.einsum("pij,pjk->pik", reach, reach, preferred_element_type=jnp.float32)
        reach = jnp.minimum(square, 1.0).astype(jnp.bfloat16)
    tree_context = jnp.einsum(
        "pkd,pde->pke", owner_query, owned_total, preferred_element_type=jnp.float32
    )
    tree_scores = jnp.einsum(
        "pkd,pmd->pkm", owner_query, owner_key, preferred_element_type=jnp.float32
    )
    tree_weights = jnp.where(reach > 0, tree_scores, 0.0).astype(jnp.bfloat16)
    tree_mixed = jnp.einsum(
        "pkm,pmd->pkd", tree_weights, owner_value, preferred_element_type=jnp.float32
    )
    node_out = head_norm(tree_context + tree_mixed).astype(jnp.bfloat16)
    gathered = lax.all_gather(node_out, "seq", axis=0, tiled=True)
    merged = (
        gathered.reshape(requests, heads_here, NODES, DH)
        .transpose(0, 2, 1, 3)
        .reshape(requests * NODES, width)
    )
    verified = lax.psum_scatter(
        jnp.dot(merged, out_weight, preferred_element_type=jnp.float32).astype(jnp.bfloat16),
        "head",
        scatter_dimension=0,
        tiled=True,
    )
    return (prefill_out, verified)


def solution(mesh):
    placed = (
        P(None, "seq", "head"),
        P(None, "seq", "head"),
        P(None, "seq", "head"),
        P(None, "head", None, None),
        P(None, "seq", "head"),
        P(None, "seq", "head"),
        P(None, "seq", "head"),
        P(),
        P("head", "seq"),
    )
    return jax.shard_map(
        on_device,
        mesh=mesh,
        in_specs=placed,
        out_specs=(P(None, "seq", "head"), P("head", "seq")),
        check_vma=False,
    )
```

profile of v0, /device:TPU:0, one launch (start us, length us, event | category | flops | bytes accessed | tf_op | source)
XLA Modules:
  0.0 203.2 jit_solution(8831126265114827285)
XLA Ops:
  7.2 0.0 copy-start
  7.2 0.0 all-gather.6.cloned.1.call-start
  7.2 6.2 %copy.85 = bf16[4,512,1024]{1,2,0:T(8,128)(2,1)} copy(bf16[4,512,1024]{2,1,0:T(8,128)(2,1)} %param.11) | data formatting | bytes 8388608 | tf_op jit(solution)/shard_map/reshape.1
  13.4 0.0 copy-start.2
  13.4 5.8 %fusion.28 = bf16[4,8,128,128]{3,2,1,0:T(8,128)(2,1)} fusion(bf16[4,512,8,128]{1,3,2,0:T(8,128)(2,1)} %bitcast.114, bf16[4,512,1024]{2,1,0:T(8,128)(2,1)} %param.10), kind=kOutput, calls=%fused_computation.43 | convolution fusion | flops 537395200 | bytes 9437184 | tf_op jit(solution)/shard_map/rnchd,rnche->rnhde/dot_general | solution.py:39
  19.2 0.0 copy-start.3
  19.2 0.0 copy-start.4
  19.2 0.0 all-gather.6.cloned.1.call-update
  19.3 0.0 copy-done.2
  19.3 0.1 copy.88
  19.4 0.9 copy.69
  20.3 5.2 %all-to-all-start = ((bf16[4,8,64,128]{3,2,1,0:T(8,128)(2,1)}), bf16[4,8,64,128]{3,2,1,0:T(8,128)(2,1)S(1)}, u32[]{:S(2)}, u32[]{:S(2)}) async-start(bf16[4,8,64,128]{3,2,1,0:T(8,128)(2,1)} %copy.69), calls=%async_computation | async-start | bytes 1048576 | tf_op jit(solution)/shard_map/all_to_all | solution.py:76
  25.5 0.0 copy-done.3
  25.5 0.1 copy.89
  25.6 0.0 copy-done.4
  25.6 0.1 copy.90
  25.7 0.0 copy-done
  25.7 0.6 gather_fusion
  26.4 0.1 broadcast_select_fusion
  26.5 3.5 %minimum_convert_fusion.6 = bf16[8,256,256]{2,1,0:T(8,128)(2,1)} fusion(s32[8,256]{1,0:T(8,128)S(1)} %broadcast_select_fusion, pred[256]{0:T(512)(128)(4,1)S(1)} %iota_compare_fusion.3, pred[256,256]{1,0:T(8,128)(4,1)S(1)} %iota_compare_fusion.2), kind=kOutput, calls=%fused_computation.36 | convolution fusion | flops 540540928 | bytes 1122560 | tf_op jit(solution)/shard_map/pij,pjk->pik/dot_general | solution.py:94
  30.0 3.7 %minimum_convert_fusion.4 = bf16[8,256,256]{2,1,0:T(8,128)(2,1)S(1)} fusion(bf16[8,256,256]{2,1,0:T(8,128)(2,1)} %minimum_convert_fusion.6), kind=kOutput, calls=%fused_computation.34 | convolution fusion | flops 538968064 | bytes 2097152 | tf_op jit(solution)/shard_map/pij,pjk->pik/dot_general | solution.py:94
  33.8 0.8 bitcast_bitcast_fusion
  34.6 0.9 copy.71
  35.5 1.0 minimum_convert_fusion.2
  36.5 0.0 all-to-all-done
  36.5 4.2 %all-to-all-start.1 = ((bf16[4,8,64,128]{3,2,1,0:T(8,128)(2,1)}), bf16[4,8,64,128]{3,2,1,0:T(8,128)(2,1)S(1)}, u32[]{:S(2)}, u32[]{:S(2)}) async-start(bf16[4,8,64,128]{3,2,1,0:T(8,128)(2,1)} %copy.71), calls=%async_computation.1 | async-start | bytes 1048576 | tf_op jit(solution)/shard_map/all_to_all | solution.py:77
  40.7 1.1 fusion.37
  41.9 8.5 %all-to-all-done.1 = bf16[4,8,64,128]{3,2,1,0:T(8,128)(2,1)S(1)} async-done(((bf16[4,8,64,128]{3,2,1,0:T(8,128)(2,1)}), bf16[4,8,64,128]{3,2,1,0:T(8,128)(2,1)S(1)}, u32[]{:S(2)}, u32[]{:S(2)}) %all-to-all-start.1) | async-done | bytes 524320 | tf_op jit(solution)/shard_map/all_to_all | solution.py:77
  50.4 4.1 %all-to-all-start.2 = ((bf16[4,8,64,128]{3,1,2,0:T(8,128)(2,1)}), bf16[4,8,64,128]{3,1,2,0:T(8,128)(2,1)}, u32[]{:S(2)}, u32[]{:S(2)}) async-start(bf16[4,8,64,128]{3,1,2,0:T(8,128)(2,1)} %bitcast_bitcast_fusion), calls=%async_computation.2 | async-start | bytes 1048576 | tf_op jit(solution)/shard_map/all_to_all | solution.py:78
  54.5 0.2 all-gather.4.cloned.1.call-start
  54.7 0.9 copy.72
  55.6 29.0 %all-gather.6.cloned.1.call-done = bf16[16,8,128,128]{3,2,1,0:T(8,128)(2,1)} async-done(((bf16[4,8,128,128]{3,2,1,0:T(8,128)(2,1)}), bf16[16,8,128,128]{3,2,1,0:T(8,128)(2,1)}) %all-gather.6.cloned.1.call-update) | async-done | bytes 4194320 | tf_op jit(solution)/shard_map/all_gather | solution.py:52
  84.6 4.2 %convert_reduce_fusion = (f32[4,8,128,128]{3,2,1,0:T(8,128)S(1)}, f32[4,8,128,128]{3,2,1,0:T(8,128)S(1)}) fusion(bf16[4,4,8,128,128]{4,3,2,1,0:T(8,128)(2,1)} %bitcast.116, pred[4]{0:T(512)(128)(4,1)S(1)} %iota_compare_fusion.4), kind=kLoop, calls=%fused_computation.6 | loop fusion | flops 7340032 | bytes 8388612 | tf_op jit(solution)/shard_map/reduce_sum | solution.py:60
  88.8 1.9 constant_dynamic-slice_fusion
  90.7 2.1 %copy.84 = f32[8,128,128]{1,2,0:T(8,128)} copy(f32[8,128,128]{2,1,0:T(8,128)} %get-tuple-element.18) | data formatting | bytes 1048576
  92.8 1.0 copy.83
  93.8 2.5 %convolution_bitcast_fusion = f32[8,256,128]{1,2,0:T(8,128)} fusion(bf16[8,256,128]{2,1,0:T(8,128)(2,1)S(1)} %bitcast.119, f32[8,128,128]{1,2,0:T(8,128)} %copy.83, f32[8,128,128]{1,2,0:T(8,128)} %copy.84), kind=kOutput, calls=%fused_computation.46 | convolution fusion | flops 67371008 | bytes 2621440 | tf_op jit(solution)/shard_map/pkd,pde->pke/dot_general | solution.py:96
  96.2 0.0 all-to-all-done.2
  96.2 3.3 %multiply_reduce_fusion = (f32[8,256]{1,0:T(8,128)S(1)}, f32[8,256,128]{1,2,0:T(8,128)}) fusion(f32[8,256,128]{1,2,0:T(8,128)} %convolution_bitcast_fusion, bf16[8,256,128]{2,0,1:T(8,128)(2,1)} %bitcast.22, bf16[8,256,128]{2,1,0:T(8,128)(2,1)S(1)} %bitcast.120, bf16[8,256,128]{2,1,0:T(8,128)(2,1)} %bitcast.131, u8[256,256]{1,0:T(8,128)(4,1)S(1)} %fusion.37), kind=kOutput, calls=%fused_computation.50 | convolution fusion | flops 272365568 | bytes 3743744 | tf_op jit(solution)/shard_map/pkm,pmd->pkd/dot_general | solution.py:103
  99.5 1.3 multiply_convert_fusion
  100.9 1.0 copy.75
  101.9 0.0 all-gather.4.cloned.1.call-update
  101.9 0.0 reduce-scatter.2.cloned.1.call-start
  101.9 35.4 %all-gather.4.cloned.1.call-done = bf16[32,256,128]{2,1,0:T(8,128)(2,1)} async-done(((bf16[8,256,128]{2,1,0:T(8,128)(2,1)}), bf16[32,256,128]{2,1,0:T(8,128)(2,1)}) %all-gather.4.cloned.1.call-update) | async-done | bytes 2097168 | tf_op jit(solution)/shard_map/all_gather | solution.py:107
  137.4 0.0 copy-start.5
  137.4 3.1 %copy.76 = bf16[4,8,256,128]{3,1,2,0:T(8,128)(2,1)S(1)} copy(bf16[4,8,256,128]{3,2,1,0:T(8,128)(2,1)} %bitcast.121) | data formatting | bytes 4194304 | tf_op jit(solution)/shard_map/reshape | solution.py:109
  140.5 0.0 copy-done.5
  140.5 6.0 %convolution_convert_fusion = bf16[1024,2048]{1,0:T(8,128)(2,1)} fusion(bf16[1024,2048]{1,0:T(8,128)(2,1)S(1)} %copy-done.5, bf16[128,8,8,128]{3,2,1,0:T(8,128)(2,1)S(1)} %bitcast.122), kind=kOutput, calls=%fused_computation.20 | convolution fusion | flops 4297064448 | bytes 10485760 | tf_op jit(solution)/shard_map/dot_general | solution.py:114
  146.5 0.0 reduce-scatter.2.cloned.1.call-update
  146.5 0.1 iota_compare_fusion.1
  146.6 15.0 %fusion = f32[4,8,512,128]{2,3,1,0:T(8,128)} fusion(bf16[4,512,8,128]{1,3,2,0:T(8,128)(2,1)} %bitcast.115, pred[512,512]{1,0:T(8,128)(4,1)S(1)} %iota_compare_fusion.1, bf16[4,512,1024]{2,1,0:T(8,128)(2,1)} %param.9, bf16[4,512,1024]{2,1,0:T(8,128)(2,1)} %param.10), kind=kOutput, calls=%fused_computation.2 | convolution fusion | flops 4311744512 | bytes 21233664 | tf_op jit(solution)/shard_map/rnhbc,rnchd->rnbhd/dot_general | solution.py:50
  161.6 10.6 %fusion.6 = (f32[4,512,8]{1,2,0:T(8,128)S(1)}, f32[4,8,128,512]{3,2,1,0:T(8,128)}) fusion(f32[4,8,512,128]{2,3,1,0:T(8,128)} %fusion, f32[4,8,128,128]{3,2,1,0:T(8,128)} %param.12, f32[4,8,128,128]{3,2,1,0:T(8,128)S(1)} %get-tuple-element.13, bf16[4,512,1024]{2,1,0:T(8,128)(2,1)} %param.9), kind=kOutput, calls=%fused_computation.11 | convolution fusion | flops 544194560 | bytes 25231360 | tf_op jit(solution)/shard_map/rnbhd,rnhde->rnbhe/dot_general | solution.py:65
  172.2 10.3 %fusion.7 = bf16[4,1,512,8,128]{2,4,3,0,1:T(8,128)(2,1)} fusion(f32[4,512,8]{1,2,0:T(8,128)S(1)} %add_rsqrt_fusion, f32[4,8,128,512]{3,2,1,0:T(8,128)} %get-tuple-element.15, f32[4,8,512,128]{2,3,1,0:T(8,128)} %fusion), kind=kLoop, calls=%fused_computation.12 | loop fusion | flops 6291456 | bytes 21037056 | tf_op jit(solution)/shard_map/convert_element_type | solution.py:68
  182.5 0.0 copy-start.1
  182.5 6.3 %copy.77 = bf16[4,512,1024]{2,1,0:T(8,128)(2,1)} copy(bf16[4,512,1024]{1,2,0:T(8,128)(2,1)} %bitcast.113) | data formatting | bytes 8388608
  188.8 7.9 %reduce-scatter.2.cloned.1.call-done = bf16[128,2048]{1,0:T(8,128)(2,1)} async-done(((bf16[1024,2048]{1,0:T(8,128)(2,1)}), bf16[128,2048]{1,0:T(8,128)(2,1)}) %reduce-scatter.2.cloned.1.call-update) | async-done | bytes 524304 | tf_op jit(solution)/shard_map/reduce_scatter | solution.py:113
  196.7 0.0 copy-done.1
  (11 shorter events, 0.2 us)
Async XLA Ops:
  7.2 18.6 %copy-start = (s32[4,256]{1,0:T(4,128)S(1)}, s32[4,256]{1,0:T(4,128)}, u32[]{:S(2)}) copy-start(s32[4,256]{1,0:T(4,128)} %param.16) | copy-start | bytes 12292
  7.2 77.4 %all-gather.6.cloned.1.call-start = ((), (), s32[]{:S(2)}) async-start(), calls=%async_computation.6 | async-start | bytes 5242880 | tf_op jit(solution)/shard_map/all_gather | solution.py:52
  13.4 5.8 %copy-start.2 = (bf16[4,64,1024]{2,1,0:T(8,128)(2,1)S(1)}, bf16[4,64,1024]{2,1,0:T(8,128)(2,1)}, u32[]{:S(2)}) copy-start(bf16[4,64,1024]{2,1,0:T(8,128)(2,1)} %param.13) | copy-start | bytes 1572868
  19.2 6.3 %copy-start.3 = (bf16[4,64,1024]{2,1,0:T(8,128)(2,1)S(1)}, bf16[4,64,1024]{2,1,0:T(8,128)(2,1)}, u32[]{:S(2)}) copy-start(bf16[4,64,1024]{2,1,0:T(8,128)(2,1)} %param.14) | copy-start | bytes 1572868
  19.2 6.4 %copy-start.4 = (bf16[4,64,1024]{2,1,0:T(8,128)(2,1)S(1)}, bf16[4,64,1024]{2,1,0:T(8,128)(2,1)}, u32[]{:S(2)}) copy-start(bf16[4,64,1024]{2,1,0:T(8,128)(2,1)} %param.15) | copy-start | bytes 1572868
  20.3 16.2 %all-to-all-start = ((bf16[4,8,64,128]{3,2,1,0:T(8,128)(2,1)}), bf16[4,8,64,128]{3,2,1,0:T(8,128)(2,1)S(1)}, u32[]{:S(2)}, u32[]{:S(2)}) async-start(bf16[4,8,64,128]{3,2,1,0:T(8,128)(2,1)} %copy.69), calls=%async_computation | async-start | bytes 1048576 | tf_op jit(solution)/shard_map/all_to_all | solution.py:76
  36.5 13.8 %all-to-all-start.1 = ((bf16[4,8,64,128]{3,2,1,0:T(8,128)(2,1)}), bf16[4,8,64,128]{3,2,1,0:T(8,128)(2,1)S(1)}, u32[]{:S(2)}, u32[]{:S(2)}) async-start(bf16[4,8,64,128]{3,2,1,0:T(8,128)(2,1)} %copy.71), calls=%async_computation.1 | async-start | bytes 1048576 | tf_op jit(solution)/shard_map/all_to_all | solution.py:77
  50.4 45.9 %all-to-all-start.2 = ((bf16[4,8,64,128]{3,1,2,0:T(8,128)(2,1)}), bf16[4,8,64,128]{3,1,2,0:T(8,128)(2,1)}, u32[]{:S(2)}, u32[]{:S(2)}) async-start(bf16[4,8,64,128]{3,1,2,0:T(8,128)(2,1)} %bitcast_bitcast_fusion), calls=%async_computation.2 | async-start | bytes 1048576 | tf_op jit(solution)/shard_map/all_to_all | solution.py:78
  54.5 82.9 %all-gather.4.cloned.1.call-start = ((), (), s32[]{:S(2)}) async-start(), calls=%async_computation.4 | async-start | bytes 2621440 | tf_op jit(solution)/shard_map/all_gather | solution.py:107
  101.9 94.8 %reduce-scatter.2.cloned.1.call-start = ((), (), s32[]{:S(2)}) async-start(), calls=%async_computation.5 | async-start | bytes 4718592 | tf_op jit(solution)/shard_map/reduce_scatter | solution.py:113
  137.4 3.1 %copy-start.5 = (bf16[1024,2048]{1,0:T(8,128)(2,1)S(1)}, bf16[1024,2048]{1,0:T(8,128)(2,1)}, u32[]{:S(2)}) copy-start(bf16[1024,2048]{1,0:T(8,128)(2,1)} %param.17) | copy-start | bytes 12582916
  182.5 14.1 %copy-start.1 = (s32[4,256]{1,0:T(4,128)S(1)}, s32[4,256]{1,0:T(4,128)}, u32[]{:S(2)}) copy-start(s32[4,256]{1,0:T(4,128)} %param.16) | copy-start | bytes 12292
Sparse Core Ops, SparseCore 0:
  19.4 65.1 all-gather.5
  102.0 35.3 all-gather.3
  146.6 49.9 reduce-scatter.1
where the time goes:
time: 204 us; the launch traced here: 203 us
  waiting for transfers between devices  80.9 us (40%)
  matrix products  52.5 us (26%)
  local copies, waits for them, and re-layouts  26 us (13%)
  other arithmetic  16 us (8%)
  between operations  13.9 us (7%)
  starting transfers between devices  13.8 us (7%)
    all_gather x1, waiting for transfers between devices, on_device(): gathered = lax.all_gather(node_out, 'seq', axis=0, tiled=True)  35.4 us
    all_gather x1, waiting for transfers between devices, on_device(): lax.all_gather(span_state[None].astype(jnp.bfloat16), 'seq', axis=0, tile...  29 us
    dot_general x1, matrix products, on_device(): jnp.einsum('rnhbc,rnchd->rnbhd', weights, v_blocks, preferred_element_typ...  15 us
    dot_general x1, matrix products, on_device(): jnp.einsum('rnbhd,rnhde->rnbhe', q_blocks, block_base, preferred_element_...  10.6 us
    convert_element_type x1, other arithmetic, on_device(): head_norm(context + inner).astype(jnp.bfloat16)  10.3 us
    unnamed x18, local copies, waits for them, and re-layouts  9.61 us
    dot_general x4, matrix products, on_device(): jnp.einsum('pij,pjk->pik', reach, reach, preferred_element_type=jnp.float32)  9.32 us
    all_to_all x1, waiting for transfers between devices, on_device(): lax.all_to_all(to_owners(tree_key), 'seq', split_axis=0, concat_axis=2, t...  8.5 us
  transfers between devices with their start and end apart: 6, of which 4 were waited for; matrix products, arithmetic and copies ran while one was open for 33% of the time, Pallas kernels for 0%

commit v1 on v0

v1 whole, which is shorter than its diff:
```python
import functools

import jax
import jax.numpy as jnp
from jax import lax
from jax.experimental import pallas as pl
from jax.experimental.pallas import tpu as pltpu
from jax.sharding import PartitionSpec as P

DH = 128
epsilon = 1e-05
VMEM_BYTES = 40 * 1024 * 1024


def head_norm(field):
    return field * lax.rsqrt(jnp.mean(field * field, axis=-1, keepdims=True) + epsilon)


def dot(a, b, over_a=1, over_b=0):
    return lax.dot_general(
        a, b, (((over_a,), (over_b,)), ((), ())), preferred_element_type=jnp.float32
    )


def columns(h):
    return slice(h * DH, (h + 1) * DH)


def kv_kernel(k_ref, v_ref, out_ref):
    for h in range(out_ref.shape[1]):
        out_ref[0, h] = dot(k_ref[0, :, columns(h)], v_ref[0, :, columns(h)], 0, 0).astype(
            jnp.bfloat16
        )


def reach_kernel(parents_ref, out_ref):
    nodes = out_ref.shape[0]
    row = lax.broadcasted_iota(jnp.int32, (nodes, nodes), 0)
    column = lax.broadcasted_iota(jnp.int32, (nodes, nodes), 1)
    links = (parents_ref[...] == column) & (row >= 1)
    reach = jnp.where(links | (row == column), 1.0, 0.0).astype(jnp.bfloat16)
    for level in range((nodes - 1).bit_length()):
        reach = jnp.minimum(dot(reach, reach), 1.0).astype(jnp.bfloat16)
    out_ref[...] = reach


def tree_kernel(pieces, qkv_ref, parts_ref, prior_ref, reach_ref, out_ref, base_ref):
    wide = pieces * DH
    reached = reach_ref[...] > 0
    for p in range(pieces):
        state = prior_ref[p]
        for s in range(parts_ref.shape[0]):
            base_ref[s, p] = state.astype(jnp.bfloat16)
            state = state + parts_ref[s, p].astype(jnp.float32)
        q = qkv_ref[:, p * DH : (p + 1) * DH]
        k = qkv_ref[:, wide + p * DH : wide + (p + 1) * DH]
        v = qkv_ref[:, 2 * wide + p * DH : 2 * wide + (p + 1) * DH]
        weights = jnp.where(reached, dot(q, k, 1, 1), 0.0).astype(jnp.bfloat16)
        raw = dot(q, state.astype(jnp.bfloat16)) + dot(weights, v)
        out_ref[:, columns(p)] = head_norm(raw).astype(jnp.bfloat16)


def prefill_kernel(heads, q_ref, k_ref, v_ref, base_ref, out_ref):
    tokens = q_ref.shape[1]
    rows = min(256, tokens)
    row = lax.broadcasted_iota(jnp.int32, (rows, rows), 0)
    column = lax.broadcasted_iota(jnp.int32, (rows, rows), 1)
    causal = row >= column
    for h in range(heads):
        for at in range(0, tokens, rows):
            q = q_ref[0, at : at + rows, columns(h)]
            raw = dot(q, base_ref[0, h])
            here = dot(q, k_ref[0, at : at + rows, columns(h)], 1, 1)
            here = jnp.where(causal, here, 0.0).astype(jnp.bfloat16)
            raw = raw + dot(here, v_ref[0, at : at + rows, columns(h)])
            if at:
                past = dot(q, k_ref[0, :at, columns(h)], 1, 1).astype(jnp.bfloat16)
                raw = raw + dot(past, v_ref[0, :at, columns(h)])
            out_ref[0, at : at + rows, columns(h)] = head_norm(raw).astype(jnp.bfloat16)


def on_device(
    query_rows,
    key_rows,
    value_rows,
    prior_state,
    tree_query,
    tree_key,
    tree_value,
    parents,
    out_weight,
):
    requests, tokens, width = query_rows.shape
    heads = width // DH
    assert tokens <= 512
    seq_index = lax.axis_index("seq")
    seq_count = lax.axis_size("seq")
    pieces = requests * heads // seq_count
    groups = heads // pieces
    assert groups * pieces == heads
    nodes_here = tree_query.shape[1]
    nodes = parents.shape[1]
    wide = pieces * DH
    params = pltpu.CompilerParams(vmem_limit_bytes=VMEM_BYTES)

    def to_owners(field):
        field = field.reshape(requests, nodes_here, groups, wide)
        return field.transpose(0, 2, 1, 3).reshape(seq_count, nodes_here, wide)

    packed = jnp.concatenate([to_owners(f) for f in (tree_query, tree_key, tree_value)], axis=2)
    owner_qkv = lax.all_to_all(packed, "seq", split_axis=0, concat_axis=0, tiled=True)
    owner_qkv = owner_qkv.reshape(nodes, 3 * wide)

    rows_spec = pl.BlockSpec((1, tokens, width), lambda r: (r, 0, 0))
    block_kv = pl.pallas_call(
        kv_kernel,
        grid=(requests,),
        in_specs=[rows_spec, rows_spec],
        out_specs=pl.BlockSpec((1, heads, DH, DH), lambda r: (r, 0, 0, 0)),
        out_shape=jax.ShapeDtypeStruct((requests, heads, DH, DH), jnp.bfloat16),
        compiler_params=params,
        cost_estimate=pl.CostEstimate(
            flops=2 * requests * tokens * width * DH,
            bytes_accessed=4 * requests * tokens * width,
            transcendentals=0,
        ),
    )(key_rows, value_rows)
    parts = lax.all_to_all(
        block_kv.reshape(seq_count, pieces, DH, DH), "seq", split_axis=0, concat_axis=0, tiled=True
    )

    own_parents = lax.dynamic_slice_in_dim(parents, seq_index // groups, 1, 0).reshape(nodes, 1)
    reach = pl.pallas_call(
        reach_kernel,
        out_shape=jax.ShapeDtypeStruct((nodes, nodes), jnp.bfloat16),
        compiler_params=params,
        cost_estimate=pl.CostEstimate(
            flops=16 * nodes**3, bytes_accessed=4 * nodes * nodes, transcendentals=0
        ),
    )(own_parents)
    flat_prior = prior_state.reshape(requests * heads, DH, DH)
    owned_prior = lax.dynamic_slice_in_dim(flat_prior, seq_index * pieces, pieces, 0)
    node_out, base = pl.pallas_call(
        functools.partial(tree_kernel, pieces),
        out_shape=(
            jax.ShapeDtypeStruct((nodes, wide), jnp.bfloat16),
            jax.ShapeDtypeStruct((seq_count, pieces, DH, DH), jnp.bfloat16),
        ),
        compiler_params=params,
        cost_estimate=pl.CostEstimate(
            flops=4 * pieces * nodes * nodes * DH,
            bytes_accessed=8 * nodes * wide + 8 * seq_count * pieces * DH * DH,
            transcendentals=0,
        ),
    )(owner_qkv, parts, owned_prior, reach)

    gathered = lax.all_gather(node_out, "seq", axis=0, tiled=True)
    merged = (
        gathered.reshape(requests, groups, nodes, wide)
        .transpose(0, 2, 1, 3)
        .reshape(requests * nodes, width)
    )
    verified = lax.psum_scatter(
        jnp.dot(merged, out_weight, preferred_element_type=jnp.float32).astype(jnp.bfloat16),
        "head",
        scatter_dimension=0,
        tiled=True,
    )

    base = lax.all_to_all(base, "seq", split_axis=0, concat_axis=0, tiled=True)
    base = base.reshape(requests, heads, DH, DH)
    step = min(4, heads)
    step_spec = pl.BlockSpec((1, tokens, step * DH), lambda r, h: (r, 0, h))
    prefill_out = pl.pallas_call(
        functools.partial(prefill_kernel, step),
        grid=(requests, heads // step),
        in_specs=[
            step_spec,
            step_spec,
            step_spec,
            pl.BlockSpec((1, step, DH, DH), lambda r, h: (r, h, 0, 0)),
        ],
        out_specs=step_spec,
        out_shape=jax.ShapeDtypeStruct((requests, tokens, width), jnp.bfloat16),
        compiler_params=params,
        cost_estimate=pl.CostEstimate(
            flops=4 * requests * tokens * tokens * width,
            bytes_accessed=8 * requests * tokens * width,
            transcendentals=0,
        ),
    )(query_rows, key_rows, value_rows, base)
    return (prefill_out, verified)


def solution(mesh):
    placed = (
        P(None, "seq", "head"),
        P(None, "seq", "head"),
        P(None, "seq", "head"),
        P(None, "head", None, None),
        P(None, "seq", "head"),
        P(None, "seq", "head"),
        P(None, "seq", "head"),
        P(),
        P("head", "seq"),
    )
    return jax.shard_map(
        on_device,
        mesh=mesh,
        in_specs=placed,
        out_specs=(P(None, "seq", "head"), P("head", "seq")),
        check_vma=False,
    )
```

time: 204 us -> 165 us (0.81)
  matrix products: 52.5 us -> 9.27 us
  Pallas kernels: 0 us -> 24.9 us
  blocking collectives: 0 us -> 16.8 us
  other arithmetic: 16 us -> 2.61 us
  waiting for transfers between devices: 80.9 us -> 69.5 us
  local copies, waits for them, and re-layouts: 26 us -> 17.9 us
  starting transfers between devices: 13.8 us -> 9.59 us
    dot_general x9 -> x0, matrix products: 46.5 us -> none  [the longest x1 15 us: on_device(): jnp.einsum('rnhbc,rnchd->rnbhd', weights, v_blocks, preferred_element_typ...]
    all_gather x1 -> x0, waiting for transfers between devices: 29 us -> none  [on_device(): lax.all_gather(span_state[None].astype(jnp.bfloat16), 'seq', axis=0, tile...]
    pallas_call x0 -> x4, Pallas kernels: none -> 24.9 us  [the longest x1 18.2 us: on_device(): pl.pallas_call(functools.partial(prefill_kernel, step), grid=(requests, h...]
    all_to_all x3 -> x2, waiting for transfers between devices: 8.5 us -> 26.5 us  [the longest x1 15.4 us: on_device(): lax.all_to_all(packed, 'seq', split_axis=0, concat_axis=0, tiled=True)]
    all_to_all x0 -> x1, blocking collectives: none -> 16.8 us  [on_device(): base = lax.all_to_all(base, 'seq', split_axis=0, concat_axis=0, tiled=True)]
    convert_element_type x2 -> x0, other arithmetic: 11.6 us -> none  [the longest x1 10.3 us: on_device(): head_norm(context + inner).astype(jnp.bfloat16)]
    unnamed x18 -> x22, local copies, waits for them, and re-layouts: 9.61 us -> 16.2 us
    another operation x1 -> x0, local copies, waits for them, and re-layouts: 6.2 us -> none
  transfers between devices with their start and end apart: 6 -> 4, of which waited for: 4 -> 4; matrix products, arithmetic and copies ran while one was open for 33% -> 3% of each run, Pallas kernels for 0% -> 12%
where the time goes in v1:
time: 165 us
  waiting for transfers between devices  69.5 us (42%)
  Pallas kernels  24.9 us (15%)
  local copies, waits for them, and re-layouts  17.9 us (11%)
  blocking collectives  16.8 us (10%)
  between operations  14.1 us (9%)
  starting transfers between devices  9.59 us (6%)
  matrix products  9.27 us (6%)
  other arithmetic  2.61 us (2%)
    all_gather x1, waiting for transfers between devices, on_device(): gathered = lax.all_gather(node_out, 'seq', axis=0, tiled=True)  35.8 us
    pallas_call x1, Pallas kernels, on_device(): pl.pallas_call(functools.partial(prefill_kernel, step), grid=(requests, h...  18.2 us
    all_to_all x1, blocking collectives, on_device(): base = lax.all_to_all(base, 'seq', split_axis=0, concat_axis=0, tiled=True)  16.8 us
    unnamed x22, local copies, waits for them, and re-layouts  16.2 us
    all_to_all x1, waiting for transfers between devices, on_device(): lax.all_to_all(packed, 'seq', split_axis=0, concat_axis=0, tiled=True)  15.4 us
    all_to_all x1, waiting for transfers between devices, on_device(): lax.all_to_all(block_kv.reshape(seq_count, pieces, DH, DH), 'seq', split_...  11 us
    dot_general x1, matrix products, on_device(): jnp.dot(merged, out_weight, preferred_element_type=jnp.float32)  9.27 us
    reduce_scatter x1, waiting for transfers between devices, on_device(): lax.psum_scatter(jnp.dot(merged, out_weight, preferred_element_type=jnp.f...  7.23 us
  transfers between devices with their start and end apart: 4, of which 4 were waited for; matrix products, arithmetic and copies ran while one was open for 3% of the time, Pallas kernels for 12%

profile of v1, /device:TPU:0, one launch (start us, length us, event | category | flops | bytes accessed | tf_op | source)
XLA Modules:
  0.0 164.7 jit_solution(16125536095565010028)
XLA Ops:
  7.2 0.0 copy-start
  7.2 0.0 copy-start.1
  7.2 2.3 %copy-done.1 = bf16[4,512,1024]{2,1,0:T(8,128)(2,1)S(1)} copy-done((bf16[4,512,1024]{2,1,0:T(8,128)(2,1)S(1)}, bf16[4,512,1024]{2,1,0:T(8,128)(2,1)}, u32[]{:S(2)}) %copy-start.1) | copy-done | bytes 4194328
  9.5 0.0 copy-start.3
  9.5 2.2 %copy-done.3 = bf16[4,512,1024]{2,1,0:T(8,128)(2,1)S(1)} copy-done((bf16[4,512,1024]{2,1,0:T(8,128)(2,1)S(1)}, bf16[4,512,1024]{2,1,0:T(8,128)(2,1)}, u32[]{:S(2)}) %copy-start.3) | copy-done | bytes 4194328
  11.7 2.1 %shard_map.104 = bf16[4,8,128,128]{3,2,1,0:T(8,128)(2,1)S(1)} custom-call(bf16[4,512,1024]{2,1,0:T(8,128)(2,1)S(1)} %copy-done.1, bf16[4,512,1024]{2,1,0:T(8,128)(2,1)S(1)} %copy-done.3), custom_call_target="tpu_custom_call" | custom-call | flops 536870912 | bytes 8388608 | tf_op jit(solution)/shard_map/pallas_call | solution.py:115
  13.8 0.0 copy-start.6
  13.8 1.0 copy-done.6
  14.8 5.2 %all-to-all-start.1 = ((bf16[4,8,128,128]{3,2,1,0:T(8,128)(2,1)}), bf16[4,8,128,128]{3,2,1,0:T(8,128)(2,1)S(1)}, u32[]{:S(2)}, u32[]{:S(2)}) async-start(bf16[4,8,128,128]{3,2,1,0:T(8,128)(2,1)} %copy-done.6), calls=%async_computation.1 | async-start | bytes 2097152 | tf_op jit(solution)/shard_map/all_to_all | solution.py:128
  20.0 2.6 %pad_maximum_fusion = bf16[4,64,3072]{2,1,0:T(8,128)(2,1)} fusion(bf16[4,64,1024]{2,1,0:T(8,128)(2,1)} %param.15, bf16[4,64,1024]{2,1,0:T(8,128)(2,1)} %param.14, bf16[4,64,1024]{2,1,0:T(8,128)(2,1)} %param.13), kind=kLoop, calls=%fused_computation.1 | loop fusion | flops 4718592 | bytes 3145728 | tf_op jit(solution)/shard_map/concatenate | solution.py:110
  22.6 11.0 %all-to-all-done.1.parts_ref = bf16[4,8,128,128]{3,2,1,0:T(8,128)(2,1)S(1)} async-done(((bf16[4,8,128,128]{3,2,1,0:T(8,128)(2,1)}), bf16[4,8,128,128]{3,2,1,0:T(8,128)(2,1)S(1)}, u32[]{:S(2)}, u32[]{:S(2)}) %all-to-all-start.1) | async-done | bytes 1048608 | tf_op jit(solution)/shard_map/all_to_all | solution.py:128
  33.6 4.3 %all-to-all-start = ((bf16[4,64,3072]{2,1,0:T(8,128)(2,1)}), bf16[4,64,3072]{2,1,0:T(8,128)(2,1)}, u32[]{:S(2)}, u32[]{:S(2)}) async-start(bf16[4,64,3072]{2,1,0:T(8,128)(2,1)} %pad_maximum_fusion), calls=%async_computation | async-start | bytes 3145728 | tf_op jit(solution)/shard_map/all_to_all | solution.py:111
  37.9 0.0 all-gather.2.cloned.1.call-start
  38.0 0.7 dynamic-slice_bitcast_fusion
  38.7 0.1 copy.11.parents_ref
  38.8 1.6 shard_map.105.reach_ref
  40.4 0.0 copy-done
  40.4 0.8 constant_dynamic-slice_fusion.prior_ref
  41.3 15.4 %all-to-all-done = bf16[4,64,3072]{2,1,0:T(8,128)(2,1)} async-done(((bf16[4,64,3072]{2,1,0:T(8,128)(2,1)}), bf16[4,64,3072]{2,1,0:T(8,128)(2,1)}, u32[]{:S(2)}, u32[]{:S(2)}) %all-to-all-start) | async-done | bytes 1572896 | tf_op jit(solution)/shard_map/all_to_all | solution.py:111
  56.7 0.0 copy-start.7
  56.7 1.0 copy-done.7
  57.8 3.1 %shard_map.106 = (bf16[256,1024]{1,0:T(8,128)(2,1)S(1)}, bf16[4,8,128,128]{3,2,1,0:T(8,128)(2,1)S(1)}) custom-call(bf16[256,3072]{1,0:T(8,128)(2,1)} %bitcast.qkv_ref, bf16[4,8,128,128]{3,2,1,0:T(8,128)(2,1)S(1)} %all-to-all-done.1.parts_ref, f32[8,128,128]{2,1,0:T(8,128)S(1)} %copy-done.7, bf16[256,256]{1,0:T(8,128)(2,1)S(1)} %shard_map.105.reach_ref), custom_call_target="tpu_custom_call" | custom-call | flops 268435456 | bytes 6291456 | tf_op jit(solution)/shard_map/pallas_call | solution.py:143
  60.8 0.0 copy-start.8
  60.8 1.0 copy-done.8
  61.8 0.0 copy-start.10
  61.8 0.8 copy-done.10
  62.6 0.0 all-gather.2.cloned.1.call-update
  62.6 0.0 reduce-scatter.2.cloned.1.call-start
  62.7 35.8 %all-gather.2.cloned.1.call-done = bf16[1024,1024]{1,0:T(8,128)(2,1)} async-done(((bf16[256,1024]{1,0:T(8,128)(2,1)}), bf16[1024,1024]{1,0:T(8,128)(2,1)}) %all-gather.2.cloned.1.call-update) | async-done | bytes 2097168 | tf_op jit(solution)/shard_map/all_gather | solution.py:157
  98.4 9.3 %convolution_convert_fusion = bf16[1024,2048]{1,0:T(8,128)(2,1)} fusion(bf16[1024,1024]{1,0:T(8,128)(2,1)} %all-gather.2.cloned.1.call-done, bf16[1024,2048]{1,0:T(8,128)(2,1)} %param.17), kind=kOutput, calls=%fused_computation | convolution fusion | flops 4297064448 | bytes 10485760 | tf_op jit(solution)/shard_map/dot_general | solution.py:164
  107.7 0.0 copy-start.9
  107.7 0.0 reduce-scatter.2.cloned.1.call-update
  107.7 1.2 copy-done.9
  108.9 16.8 %all_to_all.15.base_ref = bf16[4,8,128,128]{3,2,1,0:T(8,128)(2,1)S(1)} all-to-all(bf16[4,8,128,128]{3,2,1,0:T(8,128)(2,1)S(1)} %copy-done.9), channel_id=1, replica_groups=mesh['seq'=4,'head'=8] {'seq'}, dimensions={0} | all-to-all | bytes 2097152 | tf_op jit(solution)/shard_map/all_to_all | solution.py:170
  125.7 0.0 copy-start.2
  125.7 2.2 %copy-done.2 = bf16[4,512,1024]{2,1,0:T(8,128)(2,1)S(1)} copy-done((bf16[4,512,1024]{2,1,0:T(8,128)(2,1)S(1)}, bf16[4,512,1024]{2,1,0:T(8,128)(2,1)}, u32[]{:S(2)}) %copy-start.2) | copy-done | bytes 4194328
  128.0 0.0 copy-start.4
  128.0 2.2 %copy-done.4 = bf16[4,512,1024]{2,1,0:T(8,128)(2,1)S(1)} copy-done((bf16[4,512,1024]{2,1,0:T(8,128)(2,1)S(1)}, bf16[4,512,1024]{2,1,0:T(8,128)(2,1)}, u32[]{:S(2)}) %copy-start.4) | copy-done | bytes 4194328
  130.2 0.0 copy-start.5
  130.2 2.2 %copy-done.5 = bf16[4,512,1024]{2,1,0:T(8,128)(2,1)S(1)} copy-done((bf16[4,512,1024]{2,1,0:T(8,128)(2,1)S(1)}, bf16[4,512,1024]{2,1,0:T(8,128)(2,1)}, u32[]{:S(2)}) %copy-start.5) | copy-done | bytes 4194328
  132.5 18.2 %shard_map.107 = bf16[4,512,1024]{2,1,0:T(8,128)(2,1)} custom-call(bf16[4,512,1024]{2,1,0:T(8,128)(2,1)S(1)} %copy-done.5, bf16[4,512,1024]{2,1,0:T(8,128)(2,1)S(1)} %copy-done.2, bf16[4,512,1024]{2,1,0:T(8,128)(2,1)S(1)} %copy-done.4, bf16[4,8,128,128]{3,2,1,0:T(8,128)(2,1)S(1)} %all_to_all.15.base_ref), custom_call_target="tpu_custom_call" | custom-call | flops 4294967296 | bytes 16777216 | tf_op jit(solution)/shard_map/pallas_call | solution.py:174
  150.7 7.2 %reduce-scatter.2.cloned.1.call-done = bf16[128,2048]{1,0:T(8,128)(2,1)} async-done(((bf16[1024,2048]{1,0:T(8,128)(2,1)}), bf16[128,2048]{1,0:T(8,128)(2,1)}) %reduce-scatter.2.cloned.1.call-update) | async-done | bytes 524304 | tf_op jit(solution)/shard_map/reduce_scatter | solution.py:163
Async XLA Ops:
  7.2 33.3 %copy-start = (f32[4,8,128,128]{3,2,1,0:T(8,128)S(1)}, f32[4,8,128,128]{3,2,1,0:T(8,128)}, u32[]{:S(2)}) copy-start(f32[4,8,128,128]{3,2,1,0:T(8,128)} %param.12) | copy-start | bytes 6291460
  7.2 2.3 %copy-start.1 = (bf16[4,512,1024]{2,1,0:T(8,128)(2,1)S(1)}, bf16[4,512,1024]{2,1,0:T(8,128)(2,1)}, u32[]{:S(2)}) copy-start(bf16[4,512,1024]{2,1,0:T(8,128)(2,1)} %k_ref.3) | copy-start | bytes 12582916
  9.5 2.2 %copy-start.3 = (bf16[4,512,1024]{2,1,0:T(8,128)(2,1)S(1)}, bf16[4,512,1024]{2,1,0:T(8,128)(2,1)}, u32[]{:S(2)}) copy-start(bf16[4,512,1024]{2,1,0:T(8,128)(2,1)} %v_ref.3) | copy-start | bytes 12582916
  13.8 1.0 copy-start.6
  14.8 18.8 %all-to-all-start.1 = ((bf16[4,8,128,128]{3,2,1,0:T(8,128)(2,1)}), bf16[4,8,128,128]{3,2,1,0:T(8,128)(2,1)S(1)}, u32[]{:S(2)}, u32[]{:S(2)}) async-start(bf16[4,8,128,128]{3,2,1,0:T(8,128)(2,1)} %copy-done.6), calls=%async_computation.1 | async-start | bytes 2097152 | tf_op jit(solution)/shard_map/all_to_all | solution.py:128
  33.6 23.1 %all-to-all-start = ((bf16[4,64,3072]{2,1,0:T(8,128)(2,1)}), bf16[4,64,3072]{2,1,0:T(8,128)(2,1)}, u32[]{:S(2)}, u32[]{:S(2)}) async-start(bf16[4,64,3072]{2,1,0:T(8,128)(2,1)} %pad_maximum_fusion), calls=%async_computation | async-start | bytes 3145728 | tf_op jit(solution)/shard_map/all_to_all | solution.py:111
  37.9 60.5 %all-gather.2.cloned.1.call-start = ((), (), s32[]{:S(2)}) async-start(), calls=%async_computation.4 | async-start | bytes 2621440 | tf_op jit(solution)/shard_map/all_gather | solution.py:157
  56.7 1.0 copy-start.7
  60.8 1.0 copy-start.8
  61.8 0.8 copy-start.10
  62.6 95.3 %reduce-scatter.2.cloned.1.call-start = ((), (), s32[]{:S(2)}) async-start(), calls=%async_computation.5 | async-start | bytes 4718592 | tf_op jit(solution)/shard_map/reduce_scatter | solution.py:163
  107.7 1.2 copy-start.9
  125.7 2.2 %copy-start.2 = (bf16[4,512,1024]{2,1,0:T(8,128)(2,1)S(1)}, bf16[4,512,1024]{2,1,0:T(8,128)(2,1)}, u32[]{:S(2)}) copy-start(bf16[4,512,1024]{2,1,0:T(8,128)(2,1)} %k_ref.3) | copy-start | bytes 12582916
  128.0 2.2 %copy-start.4 = (bf16[4,512,1024]{2,1,0:T(8,128)(2,1)S(1)}, bf16[4,512,1024]{2,1,0:T(8,128)(2,1)}, u32[]{:S(2)}) copy-start(bf16[4,512,1024]{2,1,0:T(8,128)(2,1)} %v_ref.3) | copy-start | bytes 12582916
  130.2 2.2 %copy-start.5 = (bf16[4,512,1024]{2,1,0:T(8,128)(2,1)S(1)}, bf16[4,512,1024]{2,1,0:T(8,128)(2,1)}, u32[]{:S(2)}) copy-start(bf16[4,512,1024]{2,1,0:T(8,128)(2,1)} %q_ref.1) | copy-start | bytes 12582916
Sparse Core Ops, SparseCore 0:
  62.7 35.6 all-gather.1
  107.8 50.0 reduce-scatter.1
